TPU v7x, 32 devices: a whole 2x2x4 slice. The times are simulated.
32 devices in a mesh: seq: 8 (over y, x, core), head: 4 (over z).
Axes of the slice: x: 2, y: 2, z: 4, core: 2. Of those that a mesh axis runs over, the one named last changes fastest.
Arguments:
- queries: bfloat16 [2048, 64, 128], P('seq', 'head'), may hold values from -100 to 100
- key_states: bfloat16 [2048, 4, 128], P('seq'), may hold values from -6.7 to 6.7
- values: bfloat16 [2048, 4, 128], P('seq'), may hold values from -6 to 6
- grad_out: bfloat16 [2048, 64, 128], P('seq', 'head'), may hold values from -6 to 6
- picked_blocks: int32 [32, 4, 16], P('seq'), may hold values from -1 to 31, as said below
Outputs:
- grad_queries: float32 [2048, 64, 128], P('seq', 'head')
- grad_keys: float32 [2048, 4, 128], P(('seq', 'head'))
- grad_values: float32 [2048, 4, 128], P(('seq', 'head'))
Inputs may be any that keep to these rules, and one draw needn't show every extreme that they name: picked_blocks[b, g, 0] = b. The query blocks come in runs of 256 / 64 (run s holds blocks s * 4 onward); for each run s and group g, the entries j >= 1 of the run's blocks that are not -1 name blocks of distinct runs, all lower than s, and there are exactly min(s, 60) of them.
All inputs are finite; a program needn't handle non-finite values.
Results may differ from a plain program's by a relative error of at most 0.02.
Values may be sent and summed in bfloat16 or wider, within the bound.
A program may use at most 64 MiB of HBM per device.

v0:
```python
import jax
import jax.numpy as jnp
from jax import lax
from jax.sharding import PartitionSpec as P

G = 4
HPG = 16
BLK = 64
KSEL = 16


NEG = -1e30


def block_grads(operands):
    query_pair, grad_pair, key_pair, value_pair, live_pair = operands
    block_len = query_pair.shape[1]
    factor = query_pair.shape[3] ** (-0.5)
    scores = (
        jnp.einsum("athd,ajkd->ahtjk", query_pair, key_pair, preferred_element_type=jnp.float32)
        * factor
    )
    offsets = jnp.arange(block_len, dtype=jnp.int32)
    causal = offsets[None, :] <= offsets[:, None]
    leading = jnp.arange(key_pair.shape[1], dtype=jnp.int32) == 0
    visible = live_pair[:, None, None, :, None] & (
        jnp.logical_not(leading)[None, None, None, :, None] | causal[None, None, :, None, :]
    )
    scores = jnp.where(visible, scores, NEG)
    maxima = jnp.max(scores, axis=(3, 4), keepdims=True)
    weights = jnp.where(visible, jnp.exp(scores - maxima), 0.0)
    attend = weights / jnp.sum(weights, axis=(3, 4), keepdims=True)
    attend_low = attend.astype(jnp.bfloat16)
    grad_prob = jnp.einsum(
        "athe,ajke->ahtjk", grad_pair, value_pair, preferred_element_type=jnp.float32
    )
    row_dot = jnp.sum(attend * grad_prob, axis=(3, 4), keepdims=True)
    dscore = (attend * (grad_prob - row_dot)).astype(jnp.bfloat16)
    grad_query = (
        jnp.einsum("ahtjk,ajkd->athd", dscore, key_pair, preferred_element_type=jnp.float32)
        * factor
    )
    grad_key = (
        jnp.einsum("ahtjk,athd->ajkd", dscore, query_pair, preferred_element_type=jnp.float32)
        * factor
    )
    grad_value = jnp.einsum(
        "ahtjk,athe->ajke", attend_low, grad_pair, preferred_element_type=jnp.float32
    )
    return (grad_query, grad_key, grad_value)


def on_device(queries, key_states, values, grad_out, picked_blocks):
    tokens_dev, heads_dev, width_qk = queries.shape
    width_v = grad_out.shape[2]
    block_count = tokens_dev // BLK
    shard_count = lax.axis_size("seq")
    head_index = lax.axis_index("head")
    run_total = HPG // heads_dev
    group_id = head_index // run_total
    own_keys = lax.dynamic_index_in_dim(key_states, group_id, 1, keepdims=False)
    own_values = lax.dynamic_index_in_dim(values, group_id, 1, keepdims=False)
    own_picks = lax.dynamic_index_in_dim(picked_blocks, group_id, 1, keepdims=False)
    first_keys = own_keys.reshape(block_count, 1, BLK, width_qk)
    first_values = own_values.reshape(block_count, 1, BLK, width_v)
    remote = own_picks[:, 1:]
    owner_shard = jnp.where(remote >= 0, remote // block_count, -1)
    local_slot = jnp.where(remote >= 0, remote % block_count, -1)
    shard_ids = jnp.arange(shard_count, dtype=jnp.int32)
    owner_match = owner_shard[:, :, None] == shard_ids[None, None, :]
    wanted = jnp.max(jnp.where(owner_match, local_slot[:, :, None], -1), axis=(0, 1))
    asked_block = lax.all_to_all(wanted[:, None], "seq", split_axis=0, concat_axis=0, tiled=True)[
        :, 0
    ]
    chosen = (asked_block[:, None] == jnp.arange(block_count, dtype=jnp.int32)[None, :]).astype(
        jnp.bfloat16
    )
    key_rows = own_keys.reshape(block_count, BLK * width_qk)
    value_rows = own_values.reshape(block_count, BLK * width_v)
    send_keys = (
        jnp.dot(chosen, key_rows, preferred_element_type=jnp.float32)
        .astype(jnp.bfloat16)
        .reshape(shard_count, BLK, width_qk)
    )
    send_values = (
        jnp.dot(chosen, value_rows, preferred_element_type=jnp.float32)
        .astype(jnp.bfloat16)
        .reshape(shard_count, BLK, width_v)
    )
    got_keys, got_values = (
        lax.all_to_all(send_keys, "seq", split_axis=0, concat_axis=0, tiled=True),
        lax.all_to_all(send_values, "seq", split_axis=0, concat_axis=0, tiled=True),
    )
    safe_owner = jnp.maximum(owner_shard, 0)
    far_keys = jnp.take(got_keys, safe_owner, axis=0)
    far_values = jnp.take(got_values, safe_owner, axis=0)
    all_keys = jnp.concatenate([first_keys, far_keys], axis=1)
    all_values = jnp.concatenate([first_values, far_values], axis=1)
    live_slots = jnp.concatenate([jnp.ones((block_count, 1), dtype=bool), remote >= 0], axis=1)
    back_select = owner_match.reshape(block_count * (KSEL - 1), shard_count)
    pair_count = block_count // 2
    query_pairs = queries.reshape(pair_count, 2, BLK, heads_dev, width_qk)
    grad_pairs = grad_out.reshape(pair_count, 2, BLK, heads_dev, width_v)
    key_pairs = all_keys.reshape(pair_count, 2, KSEL, BLK, width_qk)
    value_pairs = all_values.reshape(pair_count, 2, KSEL, BLK, width_v)
    live_pairs = live_slots.reshape(pair_count, 2, KSEL)
    grad_query, grad_key, grad_value = lax.map(
        block_grads, (query_pairs, grad_pairs, key_pairs, value_pairs, live_pairs)
    )
    grad_queries = grad_query.reshape(tokens_dev, heads_dev, width_qk)
    grad_key = grad_key.reshape(block_count, KSEL, BLK, width_qk)
    grad_value = grad_value.reshape(block_count, KSEL, BLK, width_v)
    select_low = back_select.astype(jnp.bfloat16)
    far_key_parts = (
        grad_key[:, 1:].astype(jnp.bfloat16).reshape(block_count * (KSEL - 1), BLK * width_qk)
    )
    far_value_parts = (
        grad_value[:, 1:].astype(jnp.bfloat16).reshape(block_count * (KSEL - 1), BLK * width_v)
    )
    back_keys = (
        jnp.einsum("ps,px->sx", select_low, far_key_parts, preferred_element_type=jnp.float32)
        .astype(jnp.bfloat16)
        .reshape(shard_count, BLK, width_qk)
    )
    back_values = (
        jnp.einsum("ps,px->sx", select_low, far_value_parts, preferred_element_type=jnp.float32)
        .astype(jnp.bfloat16)
        .reshape(shard_count, BLK, width_v)
    )
    returned_keys, returned_values = (
        lax.all_to_all(back_keys, "seq", split_axis=0, concat_axis=0, tiled=True),
        lax.all_to_all(back_values, "seq", split_axis=0, concat_axis=0, tiled=True),
    )
    key_total = jnp.einsum(
        "rq,rx->qx",
        chosen,
        returned_keys.reshape(shard_count, BLK * width_qk),
        preferred_element_type=jnp.float32,
    )
    value_total = jnp.einsum(
        "rq,rx->qx",
        chosen,
        returned_values.reshape(shard_count, BLK * width_v),
        preferred_element_type=jnp.float32,
    )
    key_total = key_total + grad_key[:, 0].reshape(block_count, BLK * width_qk)
    value_total = value_total + grad_value[:, 0].reshape(block_count, BLK * width_v)
    key_total = key_total.reshape(tokens_dev, width_qk)
    value_total = value_total.reshape(tokens_dev, width_v)
    group_mask = (jnp.arange(G, dtype=jnp.int32) == group_id).astype(jnp.float32)
    key_term = key_total[:, None, :] * group_mask[None, :, None]
    value_term = value_total[:, None, :] * group_mask[None, :, None]
    grad_keys, grad_values = (
        lax.psum_scatter(key_term, "head", scatter_dimension=0, tiled=True),
        lax.psum_scatter(value_term, "head", scatter_dimension=0, tiled=True),
    )
    return (grad_queries, grad_keys, grad_values)


def solution(mesh):
    placed = (
        P("seq", "head", None),
        P("seq", None, None),
        P("seq", None, None),
        P("seq", "head", None),
        P("seq", None, None),
    )
    return jax.shard_map(
        on_device,
        mesh=mesh,
        in_specs=placed,
        out_specs=(
            P("seq", "head", None),
            P(("seq", "head"), None, None),
            P(("seq", "head"), None, None),
        ),
        check_vma=False,
    )
```

profile of v0, /device:TPU:0, one launch (start us, length us, event | category | flops | bytes accessed | tf_op | source)
XLA Modules:
  0.0 212.1 jit_solution(9833701586673273397)
XLA Ops:
  7.5 0.7 copy.58
  8.2 5.8 %all-to-all-start = ((s32[8,1,1]{2,1,0:T(1,128)}), s32[8,1,1]{2,1,0:T(1,128)S(1)}, u32[]{:S(2)}, u32[]{:S(2)}) async-start(s32[8,1,1]{2,1,0:T(1,128)} %copy.58), calls=%async_computation | async-start | bytes 8192 | tf_op jit(solution)/shard_map/all_to_all | solution.py:72
  14.0 1.3 constant_dynamic-slice_fusion.5
  15.4 3.2 %all-to-all-done = s32[8,1,1]{2,1,0:T(1,128)S(1)} async-done(((s32[8,1,1]{2,1,0:T(1,128)}), s32[8,1,1]{2,1,0:T(1,128)S(1)}, u32[]{:S(2)}, u32[]{:S(2)}) %all-to-all-start) | async-done | bytes 64 | tf_op jit(solution)/shard_map/all_to_all | solution.py:72
  18.6 0.2 reduce
  18.8 0.2 fusion.35
  19.1 0.7 copy.62
  19.8 3.4 %all-to-all-start.2 = ((bf16[8,64,128]{2,1,0:T(8,128)(2,1)}), bf16[8,64,128]{2,1,0:T(8,128)(2,1)S(1)}, u32[]{:S(2)}, u32[]{:S(2)}) async-start(bf16[8,64,128]{2,1,0:T(8,128)(2,1)} %copy.62), calls=%async_computation.2 | async-start | bytes 262144 | tf_op jit(solution)/shard_map/all_to_all | solution.py:92
  23.1 0.2 fusion.34
  23.4 0.7 copy.59
  24.0 4.6 %all-to-all-done.2 = bf16[8,64,128]{2,1,0:T(8,128)(2,1)S(1)} async-done(((bf16[8,64,128]{2,1,0:T(8,128)(2,1)}), bf16[8,64,128]{2,1,0:T(8,128)(2,1)S(1)}, u32[]{:S(2)}, u32[]{:S(2)}) %all-to-all-start.2) | async-done | bytes 131104 | tf_op jit(solution)/shard_map/all_to_all | solution.py:92
  28.6 3.4 %all-to-all-start.1 = ((bf16[8,64,128]{2,1,0:T(8,128)(2,1)}), bf16[8,64,128]{2,1,0:T(8,128)(2,1)S(1)}, u32[]{:S(2)}, u32[]{:S(2)}) async-start(bf16[8,64,128]{2,1,0:T(8,128)(2,1)} %copy.59), calls=%async_computation.1 | async-start | bytes 262144 | tf_op jit(solution)/shard_map/all_to_all | solution.py:91
  32.0 0.5 compare_convert_fusion
  32.5 0.6 eq.63
  33.2 0.7 gather_fusion.1
  34.0 3.5 %all-to-all-done.1 = bf16[8,64,128]{2,1,0:T(8,128)(2,1)S(1)} async-done(((bf16[8,64,128]{2,1,0:T(8,128)(2,1)}), bf16[8,64,128]{2,1,0:T(8,128)(2,1)S(1)}, u32[]{:S(2)}, u32[]{:S(2)}) %all-to-all-start.1) | async-done | bytes 131104 | tf_op jit(solution)/shard_map/all_to_all | solution.py:91
  37.4 0.7 gather_fusion
  38.2 0.2 broadcast_select_fusion
  38.4 1.1 pad_maximum_fusion.1
  39.6 84.2 %while.14 = (s32[]{:T(128)}, f32[2,2,64,16,128]{4,3,2,1,0:T(8,128)}, f32[2,2,16,64,128]{4,3,2,1,0:T(8,128)}, f32[2,2,16,64,128]{4,3,2,1,0:T(8,128)}, bf16[2,2,16...) while((s32[]{:T(128)}, ...), condition=%wide.region_5.7_spmd, body=%wide.region_1.6_spmd.sunk | while | flops 2745890816 | bytes 104431928 | solution.py:107
  39.9 0.1 broadcast_or_fusion.2
  40.0 0.2 broadcast_and_fusion.2
  40.2 1.4 constant_dynamic-slice_fusion.9
  41.6 3.5 %fusion.73 = (f32[2,16,64]{2,1,0:T(8,128)S(1)}, f32[2,16,64,64,16]{3,2,4,1,0:T(8,128)S(1)}) fusion(pred[2,64,16,64]{1,3,2,0:T(8,128)(4,1)S(1)} %broadcast_and_fusion.2, bf16[1,2,64,16,128]{4,3,2,1,0:T(8,128)(2,1)S(1)} %get-tuple-element.191, bf16[2,2,16,64,128]{4,3,2,1,0:T(8,128)(2,1)S(1)} %get-tuple-element.221, s32[]{:T(128)S(6)} %copy.133), kind=kOutput, calls=%fused_computation.9.clone.1 | convolution fusion | flops 543160320 | bytes 9707524 | tf_op jit(solution)/shard_map/while/body/eval_jaxpr/athd,ajkd->ahtjk/dot_general | solution.py:20
  45.1 4.5 %fusion.74 = f32[2,16,64]{2,1,0:T(8,128)S(1)} fusion(f32[2,16,64,64,16]{3,2,4,1,0:T(8,128)S(1)} %get-tuple-element.192, f32[2,16,64]{2,1,0:T(8,128)S(1)} %get-tuple-element.193, pred[2,64,16,64]{1,3,2,0:T(8,128)(4,1)S(1)} %broadcast_and_fusion.2), kind=kLoop, calls=%fused_computation.11.clone.1 | loop fusion | flops 10483712 | bytes 8536064 | tf_op jit(solution)/shard_map/while/body/eval_jaxpr/reduce_sum | solution.py:32
  49.6 6.3 %fusion.79 = f32[2,2,16,64,128]{4,3,2,1,0:T(8,128)} fusion(f32[2,2,16,64,128]{4,3,2,1,0:T(8,128)} %get-tuple-element.210, s32[]{:T(128)S(6)} %copy.133, bf16[1,2,64,16,128]{4,3,2,1,0:T(8,128)(2,1)S(1)} %get-tuple-element.194, f32[2,16,64,64,16]{3,2,4,1,0:T(8,128)S(1)} %get-tuple-element.192, f32[2,16,64]{2,1,0:T(8,128)S(1)} %fusion.74, ...), kind=kOutput, calls=%fused_computation.15.clone.1 | convolution fusion | flops 549453824 | bytes 10108932 | tf_op jit(solution)/shard_map/while/body/eval_jaxpr/ahtjk,athe->ajke/dot_general | solution.py:47
  55.9 9.8 %fusion.75 = (f32[2,16,64]{2,1,0:T(8,128)S(1)}, f32[2,16,64,64,16]{3,2,4,1,0:T(8,128)}) fusion(f32[2,16,64]{2,1,0:T(8,128)S(1)} %fusion.74, f32[2,16,64]{2,1,0:T(8,128)S(1)} %get-tuple-element.193, f32[2,16,64,64,16]{3,2,4,1,0:T(8,128)S(1)} %get-tuple-element.192, pred[2,64,16,64]{1,3,2,0:T(8,128)(4,1)S(1)} %broadcast_and_fusion.2, ...), kind=kOutput, calls=%fused_computation.4.clone.1 | convolution fusion | flops 551548928 | bytes 17981444 | tf_op jit(solution)/shard_map/while/body/eval_jaxpr/athe,ajke->ahtjk/dot_general | solution.py:34
  65.7 8.8 %fusion.76 = bf16[2,16,64,16,64]{2,4,1,3,0:T(8,128)(2,1)S(1)} fusion(f32[2,16,64,64,16]{3,2,4,1,0:T(8,128)} %get-tuple-element.195, f32[2,16,64]{2,1,0:T(8,128)S(1)} %get-tuple-element.196, f32[2,16,64]{2,1,0:T(8,128)S(1)} %fusion.74, f32[2,16,64]{2,1,0:T(8,128)S(1)} %get-tuple-element.193, f32[2,16,64,64,16]{3,2,4,1,0:T(8,128)S(1)} %get-tuple-element.192, ...), kind=kLoop, calls=%fused_computation.6.clone.1 | loop fusion | flops 16777216 | bytes 21127168 | tf_op jit(solution)/shard_map/while/body/eval_jaxpr/convert_element_type | solution.py:38
  74.5 2.5 %fusion.77 = f32[1,2,64,16,128]{4,2,3,1,0:T(8,128)S(1)} fusion(bf16[2,16,64,16,64]{2,4,1,3,0:T(8,128)(2,1)S(1)} %fusion.76, bf16[2,2,16,64,128]{4,3,2,1,0:T(8,128)(2,1)S(1)} %get-tuple-element.221, s32[]{:T(128)S(6)} %copy.133), kind=kOutput, calls=%fused_computation.18.clone.1 | convolution fusion | flops 537133056 | bytes 9961476 | tf_op jit(solution)/shard_map/while/body/eval_jaxpr/ahtjk,ajkd->athd/dot_general | solution.py:40
  77.0 2.7 %fusion.78 = f32[2,2,16,64,128]{4,3,2,1,0:T(8,128)} fusion(f32[2,2,16,64,128]{4,3,2,1,0:T(8,128)} %get-tuple-element.209, s32[]{:T(128)S(6)} %copy.133, bf16[2,16,64,16,64]{2,4,1,3,0:T(8,128)(2,1)S(1)} %fusion.76, bf16[1,2,64,16,128]{4,3,2,1,0:T(8,128)(2,1)S(1)} %get-tuple-element.191), kind=kOutput, calls=%fused_computation.22.clone.1 | convolution fusion | flops 537133056 | bytes 5767172 | tf_op jit(solution)/shard_map/while/body/eval_jaxpr/ahtjk,athd->ajkd/dot_general | solution.py:44
  79.8 0.7 copy_dynamic-update-slice_fusion.2
  80.5 1.3 copy-done.7
  82.0 0.2 broadcast_and_fusion.2
  82.2 1.4 constant_dynamic-slice_fusion.9
  83.6 3.5 %fusion.73 = (f32[2,16,64]{2,1,0:T(8,128)S(1)}, f32[2,16,64,64,16]{3,2,4,1,0:T(8,128)S(1)}) fusion(pred[2,64,16,64]{1,3,2,0:T(8,128)(4,1)S(1)} %broadcast_and_fusion.2, bf16[1,2,64,16,128]{4,3,2,1,0:T(8,128)(2,1)S(1)} %get-tuple-element.191, bf16[2,2,16,64,128]{4,3,2,1,0:T(8,128)(2,1)S(1)} %get-tuple-element.221, s32[]{:T(128)S(6)} %copy.133), kind=kOutput, calls=%fused_computation.9.clone.1 | convolution fusion | flops 543160320 | bytes 9707524 | tf_op jit(solution)/shard_map/while/body/eval_jaxpr/athd,ajkd->ahtjk/dot_general | solution.py:20
  87.0 4.5 %fusion.74 = f32[2,16,64]{2,1,0:T(8,128)S(1)} fusion(f32[2,16,64,64,16]{3,2,4,1,0:T(8,128)S(1)} %get-tuple-element.192, f32[2,16,64]{2,1,0:T(8,128)S(1)} %get-tuple-element.193, pred[2,64,16,64]{1,3,2,0:T(8,128)(4,1)S(1)} %broadcast_and_fusion.2), kind=kLoop, calls=%fused_computation.11.clone.1 | loop fusion | flops 10483712 | bytes 8536064 | tf_op jit(solution)/shard_map/while/body/eval_jaxpr/reduce_sum | solution.py:32
  91.6 6.3 %fusion.79 = f32[2,2,16,64,128]{4,3,2,1,0:T(8,128)} fusion(f32[2,2,16,64,128]{4,3,2,1,0:T(8,128)} %get-tuple-element.210, s32[]{:T(128)S(6)} %copy.133, bf16[1,2,64,16,128]{4,3,2,1,0:T(8,128)(2,1)S(1)} %get-tuple-element.194, f32[2,16,64,64,16]{3,2,4,1,0:T(8,128)S(1)} %get-tuple-element.192, f32[2,16,64]{2,1,0:T(8,128)S(1)} %fusion.74, ...), kind=kOutput, calls=%fused_computation.15.clone.1 | convolution fusion | flops 549453824 | bytes 10108932 | tf_op jit(solution)/shard_map/while/body/eval_jaxpr/ahtjk,athe->ajke/dot_general | solution.py:47
  97.9 9.8 %fusion.75 = (f32[2,16,64]{2,1,0:T(8,128)S(1)}, f32[2,16,64,64,16]{3,2,4,1,0:T(8,128)}) fusion(f32[2,16,64]{2,1,0:T(8,128)S(1)} %fusion.74, f32[2,16,64]{2,1,0:T(8,128)S(1)} %get-tuple-element.193, f32[2,16,64,64,16]{3,2,4,1,0:T(8,128)S(1)} %get-tuple-element.192, pred[2,64,16,64]{1,3,2,0:T(8,128)(4,1)S(1)} %broadcast_and_fusion.2, ...), kind=kOutput, calls=%fused_computation.4.clone.1 | convolution fusion | flops 551548928 | bytes 17981444 | tf_op jit(solution)/shard_map/while/body/eval_jaxpr/athe,ajke->ahtjk/dot_general | solution.py:34
  107.7 8.8 %fusion.76 = bf16[2,16,64,16,64]{2,4,1,3,0:T(8,128)(2,1)S(1)} fusion(f32[2,16,64,64,16]{3,2,4,1,0:T(8,128)} %get-tuple-element.195, f32[2,16,64]{2,1,0:T(8,128)S(1)} %get-tuple-element.196, f32[2,16,64]{2,1,0:T(8,128)S(1)} %fusion.74, f32[2,16,64]{2,1,0:T(8,128)S(1)} %get-tuple-element.193, f32[2,16,64,64,16]{3,2,4,1,0:T(8,128)S(1)} %get-tuple-element.192, ...), kind=kLoop, calls=%fused_computation.6.clone.1 | loop fusion | flops 16777216 | bytes 21127168 | tf_op jit(solution)/shard_map/while/body/eval_jaxpr/convert_element_type | solution.py:38
  116.5 2.5 %fusion.77 = f32[1,2,64,16,128]{4,2,3,1,0:T(8,128)S(1)} fusion(bf16[2,16,64,16,64]{2,4,1,3,0:T(8,128)(2,1)S(1)} %fusion.76, bf16[2,2,16,64,128]{4,3,2,1,0:T(8,128)(2,1)S(1)} %get-tuple-element.221, s32[]{:T(128)S(6)} %copy.133), kind=kOutput, calls=%fused_computation.18.clone.1 | convolution fusion | flops 537133056 | bytes 9961476 | tf_op jit(solution)/shard_map/while/body/eval_jaxpr/ahtjk,ajkd->athd/dot_general | solution.py:40
  119.0 2.7 %fusion.78 = f32[2,2,16,64,128]{4,3,2,1,0:T(8,128)} fusion(f32[2,2,16,64,128]{4,3,2,1,0:T(8,128)} %get-tuple-element.209, s32[]{:T(128)S(6)} %copy.133, bf16[2,16,64,16,64]{2,4,1,3,0:T(8,128)(2,1)S(1)} %fusion.76, bf16[1,2,64,16,128]{4,3,2,1,0:T(8,128)(2,1)S(1)} %get-tuple-element.191), kind=kOutput, calls=%fused_computation.22.clone.1 | convolution fusion | flops 537133056 | bytes 5767172 | tf_op jit(solution)/shard_map/while/body/eval_jaxpr/ahtjk,athd->ajkd/dot_general | solution.py:44
  121.8 0.7 copy_dynamic-update-slice_fusion.2
  122.5 1.3 copy-done.7
  123.8 0.9 slice_bitcast_fusion
  124.7 1.7 slice.46
  126.5 0.9 slice_bitcast_fusion.1
  127.4 1.7 slice.47
  129.2 0.7 copy.92
  130.0 0.4 fusion.33
  130.3 0.7 copy.69
  131.0 3.4 %all-to-all-start.4 = ((bf16[8,64,128]{2,1,0:T(8,128)(2,1)}), bf16[8,64,128]{2,1,0:T(8,128)(2,1)S(1)}, u32[]{:S(2)}, u32[]{:S(2)}) async-start(bf16[8,64,128]{2,1,0:T(8,128)(2,1)} %copy.69), calls=%async_computation.4 | async-start | bytes 262144 | tf_op jit(solution)/shard_map/all_to_all | solution.py:132
  134.5 0.7 copy.89
  135.2 0.4 fusion.32
  135.6 0.7 copy.67
  136.3 3.6 %all-to-all-done.4 = bf16[8,64,128]{2,1,0:T(8,128)(2,1)S(1)} async-done(((bf16[8,64,128]{2,1,0:T(8,128)(2,1)}), bf16[8,64,128]{2,1,0:T(8,128)(2,1)S(1)}, u32[]{:S(2)}, u32[]{:S(2)}) %all-to-all-start.4) | async-done | bytes 131104 | tf_op jit(solution)/shard_map/all_to_all | solution.py:132
  139.9 3.4 %all-to-all-start.3 = ((bf16[8,64,128]{2,1,0:T(8,128)(2,1)}), bf16[8,64,128]{2,1,0:T(8,128)(2,1)S(1)}, u32[]{:S(2)}, u32[]{:S(2)}) async-start(bf16[8,64,128]{2,1,0:T(8,128)(2,1)} %copy.67), calls=%async_computation.3 | async-start | bytes 262144 | tf_op jit(solution)/shard_map/all_to_all | solution.py:131
  143.3 0.3 convolution_add_fusion
  143.7 5.0 %all-to-all-done.3 = bf16[8,64,128]{2,1,0:T(8,128)(2,1)S(1)} async-done(((bf16[8,64,128]{2,1,0:T(8,128)(2,1)}), bf16[8,64,128]{2,1,0:T(8,128)(2,1)S(1)}, u32[]{:S(2)}, u32[]{:S(2)}) %all-to-all-start.3) | async-done | bytes 131104 | tf_op jit(solution)/shard_map/all_to_all | solution.py:131
  148.7 0.3 convolution_add_fusion.1
  149.1 1.2 broadcast_multiply_fusion
  150.4 0.6 dynamic-slice
  151.6 50.5 %all-reduce.6.cloned.1.call-done = (f32[256,4,128]{2,1,0:T(4,128)}, f32[256,4,128]{2,1,0:T(4,128)}) async-done(((f32[256,4,128]{2,1,0:T(4,128)}, f32[256,4,128]{2,1,0:T(4,128)}), (f32[256,4,128]{2,1,0:T(4,128)}, f32[256,4,128]{2,1,0:T(4,128)})) %all-reduce.6.cloned.1.call-update) | async-done | bytes 1048592
  202.1 1.6 constant_dynamic-slice_fusion.4
  203.7 1.6 constant_dynamic-slice_fusion.3
  (49 shorter events, 1.3 us)
Async XLA Ops:
  8.2 10.4 %all-to-all-start = ((s32[8,1,1]{2,1,0:T(1,128)}), s32[8,1,1]{2,1,0:T(1,128)S(1)}, u32[]{:S(2)}, u32[]{:S(2)}) async-start(s32[8,1,1]{2,1,0:T(1,128)} %copy.58), calls=%async_computation | async-start | bytes 8192 | tf_op jit(solution)/shard_map/all_to_all | solution.py:72
  18.8 20.7 %copy-start.2 = (s32[8]{0:T(128)}, s32[8]{0:T(128)S(1)}, u32[]{:S(2)}) copy-start(s32[8]{0:T(128)S(1)} %reduce) | copy-start | bytes 100
  19.8 8.8 %all-to-all-start.2 = ((bf16[8,64,128]{2,1,0:T(8,128)(2,1)}), bf16[8,64,128]{2,1,0:T(8,128)(2,1)S(1)}, u32[]{:S(2)}, u32[]{:S(2)}) async-start(bf16[8,64,128]{2,1,0:T(8,128)(2,1)} %copy.62), calls=%async_computation.2 | async-start | bytes 262144 | tf_op jit(solution)/shard_map/all_to_all | solution.py:92
  28.6 8.8 %all-to-all-start.1 = ((bf16[8,64,128]{2,1,0:T(8,128)(2,1)}), bf16[8,64,128]{2,1,0:T(8,128)(2,1)S(1)}, u32[]{:S(2)}, u32[]{:S(2)}) async-start(bf16[8,64,128]{2,1,0:T(8,128)(2,1)} %copy.59), calls=%async_computation.1 | async-start | bytes 262144 | tf_op jit(solution)/shard_map/all_to_all | solution.py:91
  39.6 90.3 %copy-start.4 = (s32[60]{0:T(128)S(1)}, s32[60]{0:T(128)}, u32[]{:S(2)}) copy-start(s32[60]{0:T(128)} %eq.63) | copy-start | bytes 724
  39.6 103.7 %copy-start.3 = (s32[8]{0:T(128)S(1)}, s32[8]{0:T(128)}, u32[]{:S(2)}) copy-start(s32[8]{0:T(128)} %copy-done.2) | copy-start | bytes 100
  74.5 5.2 %copy-start.6 = (f32[2,2,64,16,128]{4,3,2,1,0:T(8,128)S(1)}, f32[2,2,64,16,128]{4,3,2,1,0:T(8,128)}, u32[]{:S(2)}) copy-start(f32[2,2,64,16,128]{4,3,2,1,0:T(8,128)} %get-tuple-element.208) | copy-start | bytes 6291460 | tf_op jit(solution)/shard_map/while
  80.5 1.3 copy-start.7
  116.5 5.3 %copy-start.6 = (f32[2,2,64,16,128]{4,3,2,1,0:T(8,128)S(1)}, f32[2,2,64,16,128]{4,3,2,1,0:T(8,128)}, u32[]{:S(2)}) copy-start(f32[2,2,64,16,128]{4,3,2,1,0:T(8,128)} %get-tuple-element.208) | copy-start | bytes 6291460 | tf_op jit(solution)/shard_map/while
  122.5 1.3 copy-start.7
  123.8 25.3 %copy-start.5 = (f32[4]{0:T(128)S(1)}, f32[4]{0:T(128)}, u32[]{:S(2)}) copy-start(f32[4]{0:T(128)} %compare_convert_fusion) | copy-start | bytes 52
  123.8 26.6 %copy-start.8 = (u32[32]{0:T(128)S(1)}, u32[32]{0:T(128)}, u32[]{:S(2)}) copy-start(u32[32]{0:T(128)} %constant.111) | copy-start | bytes 388
  123.8 81.5 %copy-start.1 = (s32[4,4,16]{2,1,0:T(4,128)S(1)}, s32[4,4,16]{2,1,0:T(4,128)}, u32[]{:S(2)}) copy-start(s32[4,4,16]{2,1,0:T(4,128)} %param.13) | copy-start | bytes 3076
  131.0 8.8 %all-to-all-start.4 = ((bf16[8,64,128]{2,1,0:T(8,128)(2,1)}), bf16[8,64,128]{2,1,0:T(8,128)(2,1)S(1)}, u32[]{:S(2)}, u32[]{:S(2)}) async-start(bf16[8,64,128]{2,1,0:T(8,128)(2,1)} %copy.69), calls=%async_computation.4 | async-start | bytes 262144 | tf_op jit(solution)/shard_map/all_to_all | solution.py:132
  139.9 8.8 %all-to-all-start.3 = ((bf16[8,64,128]{2,1,0:T(8,128)(2,1)}), bf16[8,64,128]{2,1,0:T(8,128)(2,1)S(1)}, u32[]{:S(2)}, u32[]{:S(2)}) async-start(bf16[8,64,128]{2,1,0:T(8,128)(2,1)} %copy.67), calls=%async_computation.3 | async-start | bytes 262144 | tf_op jit(solution)/shard_map/all_to_all | solution.py:131
  143.2 58.9 %all-reduce.6.cloned.1.call-start = ((), (), s32[]{:S(2)}) async-start(), calls=%async_computation.5 | async-start | bytes 2097152
  (1 other events, 0.0 us)
Sparse Core Ops, SparseCore 0:
  150.5 51.5 all-reduce.5
where the time goes:
time: 213 us; the launch traced here: 212 us
  waiting for transfers between devices  70.2 us (33%)
  matrix products  51.5 us (24%)
  other arithmetic  31 us (15%)
  local copies, waits for them, and re-layouts  24.7 us (12%)
  starting transfers between devices  19.4 us (9%)
  between operations  15 us (7%)
    unnamed x2, waiting for transfers between devices  50.5 us
    dot_general x2, matrix products, block_grads(): jnp.einsum('athe,ajke->ahtjk', grad_pair, value_pair, preferred_element_t...  19.7 us
    convert_element_type x2, other arithmetic, block_grads(): dscore = (attend * (grad_prob - row_dot)).astype(jnp.bfloat16)  17.6 us
    dot_general x2, matrix products, block_grads(): jnp.einsum('ahtjk,athe->ajke', attend_low, grad_pair, preferred_element_t...  12.6 us
    reduce_sum x2, other arithmetic, block_grads(): attend = weights / jnp.sum(weights, axis=(3, 4), keepdims=True)  9.06 us
    unnamed x25, local copies, waits for them, and re-layouts  7.24 us
    dot_general x2, matrix products, block_grads(): jnp.einsum('athd,ajkd->ahtjk', query_pair, key_pair, preferred_element_ty...  6.93 us
    all_to_all x1, starting transfers between devices, on_device(): lax.all_to_all(wanted[:, None], 'seq', split_axis=0, concat_axis=0, tiled...  5.84 us
  transfers between devices with their start and end apart: 6, of which 6 were waited for; matrix products, arithmetic and copies ran while one was open for 3% of the time, Pallas kernels for 0%

commit v1 on v0

v1 whole, which is shorter than its diff:
```python
import functools
import math

import jax
import jax.numpy as jnp
from jax import lax
from jax.experimental import pallas as pl
from jax.experimental.pallas import tpu as pltpu
from jax.sharding import PartitionSpec as P

G = 4
HPG = 16
BLK = 64
NEG = -1e30
MESH = pl.DeviceIdType.MESH
F32 = jnp.float32
BF16 = jnp.bfloat16
NT = (((1,), (1,)), ((), ()))


def kernel(
    shards, peers, heads_dev, chunk,
    q_hbm, go_hbm, kv_ref, wanted_ref, bias_ref,
    dq_hbm, out_ref,
    q_buf, go_buf, dq_buf, slots, key_t, bias_buf, acc, own,
    ask_out, ask_in, kv_out, ret_out, ret_in, hx_out, hx_in,
    load_sem, dq_sem, ask_ssem, ask_rsem, kv_ssem, kv_rsem,
    ret_ssem, ret_rsem, hx_ssem, hx_rsem,
):
    me = lax.axis_index("seq")
    mh = lax.axis_index("head")
    width = q_hbm.shape[1]
    factor = width ** (-0.5)
    blocks = kv_ref.shape[1] // BLK
    rows_b = q_buf.shape[0] // blocks
    part = kv_ref.shape[1] // peers
    run_total = HPG // heads_dev

    def at_block(i):
        return pl.ds(pl.multiple_of(i * BLK, BLK), BLK)

    def seq_copy(src, dst, ssem, rsem, peer):
        return pltpu.make_async_remote_copy(
            src_ref=src, dst_ref=dst, send_sem=ssem, recv_sem=rsem,
            device_id=(peer, mh), device_id_type=MESH,
        )

    def ask_copy(src_at, to, frm):
        return seq_copy(ask_out.at[src_at], ask_in.at[frm], ask_ssem.at[src_at], ask_rsem.at[frm], to)

    def kv_copy(src_at, to, frm):
        return seq_copy(
            kv_out.at[src_at], slots.at[:, at_block(frm)], kv_ssem.at[src_at], kv_rsem.at[frm], to
        )

    def ret_copy(src_at, to, frm):
        return seq_copy(ret_out.at[src_at], ret_in.at[frm], ret_ssem.at[src_at], ret_rsem.at[frm], to)

    def hx_copy(src_at, to, frm):
        return pltpu.make_async_remote_copy(
            src_ref=hx_out.at[src_at], dst_ref=hx_in.at[frm],
            send_sem=hx_ssem.at[src_at], recv_sem=hx_rsem.at[frm],
            device_id=(me, to), device_id_type=MESH,
        )

    load_q = pltpu.make_async_copy(q_hbm, q_buf, load_sem.at[0])
    load_go = pltpu.make_async_copy(go_hbm, go_buf, load_sem.at[1])
    load_q.start()
    load_go.start()

    barrier = pltpu.get_barrier_semaphore()

    @pl.loop(0, shards)
    def _(i):
        @pl.when(i != me)
        def _():
            pl.semaphore_signal(barrier, inc=1, device_id=(i, mh), device_id_type=MESH)

    @pl.loop(0, peers)
    def _(i):
        @pl.when(i != mh)
        def _():
            pl.semaphore_signal(barrier, inc=1, device_id=(me, i), device_id_type=MESH)

    @pl.loop(0, shards)
    def _(i):
        ask_out[i] = jnp.full((8, 128), wanted_ref[i], jnp.int32)

        @pl.when(i > me)
        def _():
            slots[:, at_block(i)] = jnp.zeros((2, BLK, width), BF16)

    pl.semaphore_wait(barrier, shards + peers - 2)

    @pl.loop(0, shards)
    def _(i):
        @pl.when(i < me)
        def _():
            ask_copy(i, i, me).start()

    acc[...] = jnp.zeros(acc.shape, F32)

    @pl.loop(0, shards)
    def _(i):
        @pl.when(i > me)
        def _():
            ask_copy(i, i, i).wait_recv()
            asked = ask_in[i][0:1, :]
            total = jnp.zeros((2, BLK, width), F32)
            for q in range(blocks):
                hit = (asked == q).astype(F32)
                total = total + kv_ref[:, q * BLK : (q + 1) * BLK].astype(F32) * hit[None]
            kv_out[i] = total.astype(BF16)
            kv_copy(i, i, me).start()

    load_q.wait()
    load_go.wait()

    @pl.loop(0, shards)
    def _(i):
        @pl.when(i < me)
        def _():
            kv_copy(i, i, i).wait_recv()

    scale = factor * math.log2(math.e)

    @pl.loop(0, blocks)
    def _(b):
        slots[:, at_block(me)] = kv_ref[:, at_block(b)]
        acc[:, at_block(me)] = jnp.zeros((2, BLK, width), F32)

        @pl.loop(0, shards)
        def _(i):
            bias_buf[at_block(i)] = jnp.full((BLK, chunk), bias_ref[b, i], F32)

        key_t[...] = slots[0].T

        @pl.loop(0, rows_b // chunk)
        def _(c):
            rows = pl.ds(pl.multiple_of(b * rows_b + c * chunk, chunk), chunk)
            key_row = lax.broadcasted_iota(jnp.int32, (BLK, chunk), 0)
            lane = lax.broadcasted_iota(jnp.int32, (BLK, chunk), 1)
            bias_buf[at_block(me)] = jnp.where(key_row * heads_dev <= lane + c * chunk, 0.0, NEG)
            qc = q_buf[rows]
            gc = go_buf[rows]
            s = lax.dot_general(slots[0], qc, NT, preferred_element_type=F32)
            s = s * scale + bias_buf[...]
            p = jnp.exp2(s - jnp.max(s, axis=0, keepdims=True))
            inverse = 1.0 / jnp.sum(p, axis=0, keepdims=True)
            a = p * inverse
            gp = lax.dot_general(slots[1], gc, NT, preferred_element_type=F32)
            row_dot = jnp.sum(a * gp, axis=0, keepdims=True)
            ds = (a * (gp - row_dot)).astype(BF16)
            acc[1] += jnp.dot(a.astype(BF16), gc, preferred_element_type=F32)
            acc[0] += jnp.dot(ds, qc, preferred_element_type=F32)
            dq_t = jnp.dot(key_t[...], ds, preferred_element_type=F32)
            dq_buf[rows] = (dq_t * factor).T

        own[0, at_block(b)] = acc[0, at_block(me)] * factor
        own[1, at_block(b)] = acc[1, at_block(me)]
        rows = pl.ds(pl.multiple_of(b * rows_b, rows_b), rows_b)
        pltpu.make_async_copy(dq_buf.at[rows], dq_hbm.at[rows], dq_sem.at[b]).start()

    @pl.loop(0, shards)
    def _(i):
        @pl.when(i < me)
        def _():
            ret_out[i, 0] = (acc[0, at_block(i)] * factor).astype(BF16)
            ret_out[i, 1] = acc[1, at_block(i)].astype(BF16)
            ret_copy(i, i, me).start()

    @pl.loop(0, shards)
    def _(i):
        @pl.when(i > me)
        def _():
            ret_copy(i, i, i).wait_recv()
            asked = ask_in[i][0:1, :]
            back = ret_in[i].astype(F32)
            for q in range(blocks):
                hit = (asked == q).astype(F32)
                own[:, q * BLK : (q + 1) * BLK] += back * hit[None]

    @pl.loop(0, peers)
    def _(i):
        @pl.when(i != mh)
        def _():
            hx_out[i] = own[:, pl.ds(pl.multiple_of(i * part, part), part)].astype(BF16)
            hx_copy(i, i, mh).start()

    hx_in[mh] = own[:, pl.ds(pl.multiple_of(mh * part, part), part)].astype(BF16)

    @pl.loop(0, peers)
    def _(i):
        @pl.when(i != mh)
        def _():
            hx_copy(i, i, i).wait_recv()

    for g in range(G):
        total = hx_in[g * run_total].astype(F32)
        for c in range(1, run_total):
            total = total + hx_in[g * run_total + c].astype(F32)
        out_ref[:, g] = total

    @pl.loop(0, shards)
    def _(i):
        @pl.when(i < me)
        def _():
            ask_copy(i, i, me).wait_send()
            ret_copy(i, i, me).wait_send()

        @pl.when(i > me)
        def _():
            kv_copy(i, i, me).wait_send()

    @pl.loop(0, peers)
    def _(i):
        @pl.when(i != mh)
        def _():
            hx_copy(i, i, mh).wait_send()

    @pl.loop(0, blocks)
    def _(b):
        rows = pl.ds(pl.multiple_of(b * rows_b, rows_b), rows_b)
        pltpu.make_async_copy(dq_buf.at[rows], dq_hbm.at[rows], dq_sem.at[b]).wait()


def on_device(queries, key_states, values, grad_out, picked_blocks):
    tokens_dev, heads_dev, width = queries.shape
    blocks = tokens_dev // BLK
    shards = lax.axis_size("seq")
    peers = lax.axis_size("head")
    me = lax.axis_index("seq")
    group_id = lax.axis_index("head") // (HPG // heads_dev)
    kv = jnp.stack([
        lax.dynamic_index_in_dim(key_states, group_id, 1, keepdims=False),
        lax.dynamic_index_in_dim(values, group_id, 1, keepdims=False),
    ])
    picks = lax.dynamic_index_in_dim(picked_blocks, group_id, 1, keepdims=False)[:, 1:]
    shard_ids = jnp.arange(shards, dtype=jnp.int32)
    match = (picks >= 0)[:, :, None] & ((picks // blocks)[:, :, None] == shard_ids)
    wanted = jnp.max(jnp.where(match, (picks % blocks)[:, :, None], -1), axis=(0, 1))
    bias = jnp.where(jnp.any(match, axis=1) | (shard_ids == me), 0.0, NEG).astype(F32)
    rows = tokens_dev * heads_dev
    chunk = min(256, rows // blocks)
    part = tokens_dev // peers
    keys = shards * BLK
    dma = pltpu.SemaphoreType.DMA
    any_spec = pl.BlockSpec(memory_space=pl.ANY)
    vmem = pl.BlockSpec(memory_space=pltpu.VMEM)
    smem = pl.BlockSpec(memory_space=pltpu.SMEM)
    dq, out = pl.pallas_call(
        functools.partial(kernel, shards, peers, heads_dev, chunk),
        out_shape=(
            jax.ShapeDtypeStruct((rows, width), F32),
            jax.ShapeDtypeStruct((2, G, part, width), F32),
        ),
        in_specs=[any_spec, any_spec, vmem, smem, smem],
        out_specs=(any_spec, vmem),
        scratch_shapes=[
            pltpu.VMEM((rows, width), BF16),
            pltpu.VMEM((rows, width), BF16),
            pltpu.VMEM((rows, width), F32),
            pltpu.VMEM((2, keys, width), BF16),
            pltpu.VMEM((width, keys), BF16),
            pltpu.VMEM((keys, chunk), F32),
            pltpu.VMEM((2, keys, width), F32),
            pltpu.VMEM((2, tokens_dev, width), F32),
            pltpu.VMEM((shards, 8, 128), jnp.int32),
            pltpu.VMEM((shards, 8, 128), jnp.int32),
            pltpu.VMEM((shards, 2, BLK, width), BF16),
            pltpu.VMEM((shards, 2, BLK, width), BF16),
            pltpu.VMEM((shards, 2, BLK, width), BF16),
            pltpu.VMEM((peers, 2, part, width), BF16),
            pltpu.VMEM((peers, 2, part, width), BF16),
            dma((2,)), dma((blocks,)),
            dma((shards,)), dma((shards,)), dma((shards,)), dma((shards,)),
            dma((shards,)), dma((shards,)), dma((peers,)), dma((peers,)),
        ],
        compiler_params=pltpu.CompilerParams(
            collective_id=0, has_side_effects=True, vmem_limit_bytes=48 * 1024 * 1024
        ),
    )(queries.reshape(rows, width), grad_out.reshape(rows, width), kv, wanted, bias)
    return (
        dq.reshape(tokens_dev, heads_dev, width),
        out[0].transpose(1, 0, 2),
        out[1].transpose(1, 0, 2),
    )


def solution(mesh):
    placed = (
        P("seq", "head", None),
        P("seq", None, None),
        P("seq", None, None),
        P("seq", "head", None),
        P("seq", None, None),
    )
    return jax.shard_map(
        on_device,
        mesh=mesh,
        in_specs=placed,
        out_specs=(
            P("seq", "head", None),
            P(("seq", "head"), None, None),
            P(("seq", "head"), None, None),
        ),
        check_vma=False,
    )
```

time: 213 us -> 45.6 us (0.21)
  waiting for transfers between devices: 70.2 us -> 0 us
  matrix products: 51.5 us -> 0 us
  Pallas kernels: 0 us -> 37.5 us
  other arithmetic: 31 us -> 0.53 us
  starting transfers between devices: 19.4 us -> 0 us
  local copies, waits for them, and re-layouts: 24.7 us -> 6.62 us
  between operations: 15 us -> 0.73 us
    dot_general x16 -> x0, matrix products: 51.5 us -> none  [the longest x2 19.7 us: block_grads(): jnp.einsum('athe,ajke->ahtjk', grad_pair, value_pair, preferred_element_t...]
    unnamed x2 -> x0, waiting for transfers between devices: 50.5 us -> none
    pallas_call x0 -> x1, Pallas kernels: none -> 37.5 us  [on_device(): pl.pallas_call(functools.partial(kernel, shards, peers, heads_dev, chunk)...]
    all_to_all x5 -> x0, waiting for transfers between devices: 19.8 us -> none  [the longest x1 4.98 us: on_device(): lax.all_to_all(back_keys, 'seq', split_axis=0, concat_axis=0, tiled=True)]
    all_to_all x5 -> x0, starting transfers between devices: 19.3 us -> none  [the longest x1 5.84 us: on_device(): lax.all_to_all(wanted[:, None], 'seq', split_axis=0, concat_axis=0, tiled...]
    convert_element_type x3 -> x0, other arithmetic: 18.1 us -> none  [the longest x2 17.6 us: block_grads(): dscore = (attend * (grad_prob - row_dot)).astype(jnp.bfloat16)]
    reduce_sum x2 -> x0, other arithmetic: 9.06 us -> none  [block_grads(): attend = weights / jnp.sum(weights, axis=(3, 4), keepdims=True)]
    slice x2 -> x0, local copies, waits for them, and re-layouts: 3.45 us -> none  [the longest x1 1.73 us: on_device(): grad_key[:, 1:].astype(jnp.bfloat16)]
  transfers between devices with their start and end apart: 6 -> 0, of which waited for: 6 -> 0; matrix products, arithmetic and copies ran while one was open for 3% -> 0% of each run, Pallas kernels for 0% -> 0%
where the time goes in v1:
time: 45.6 us; the launch traced here: 45.4 us
  Pallas kernels  37.5 us (82%)
  local copies, waits for them, and re-layouts  6.62 us (15%)
  between operations  0.73 us (2%)
  other arithmetic  0.53 us (1%)
    pallas_call x1, Pallas kernels, on_device(): pl.pallas_call(functools.partial(kernel, shards, peers, heads_dev, chunk)...  37.5 us
    unnamed x11, local copies, waits for them, and re-layouts  5.28 us
    dynamic_slice x1, local copies, waits for them, and re-layouts, on_device(): lax.dynamic_index_in_dim(values, group_id, 1, keepdims=False)  1.31 us

profile of v1, /device:TPU:0, one launch (start us, length us, event | category | flops | bytes accessed | tf_op | source)
XLA Modules:
  0.0 45.4 jit_solution(4498483240231436328)
XLA Ops:
  0.6 0.0 copy-start
  0.7 0.0 copy-done
  0.7 0.1 slice_compare_fusion.1
  0.8 0.1 add_select_fusion.1
  0.8 0.1 add_select_fusion
  0.9 0.1 select_reduce_fusion.wanted_ref
  1.0 0.1 fusion.1
  1.2 1.3 %constant_dynamic-slice_fusion.1 = (bf16[256,1,128]{2,1,0:T(2,128)(2,1)S(1)}, bf16[256,1,128]{2,1,0:T(2,128)(2,1)S(1)}) fusion(bf16[256,4,128]{2,1,0:T(4,128)(2,1)} %param.7, s32[]{:T(128)S(6)} %select_n.29, bf16[256,4,128]{2,1,0:T(4,128)(2,1)} %param.6), kind=kLoop, calls=%fused_computation.21 | loop fusion | bytes 262148 | tf_op jit(solution)/shard_map/jit(dynamic_index_in_dim)/dynamic_slice | solution.py:236
  2.6 0.0 copy-start.1
  2.6 1.2 %copy-done.1 = bf16[256,16,128]{2,1,0:T(8,128)(2,1)S(1)} copy-done((bf16[256,16,128]{2,1,0:T(8,128)(2,1)S(1)}, bf16[256,16,128]{2,1,0:T(8,128)(2,1)}, u32[]{:S(2)}) %copy-start.1) | copy-done | bytes 1048600
  3.8 0.0 copy-start.2
  3.8 1.2 %copy-done.2 = bf16[256,16,128]{2,1,0:T(8,128)(2,1)S(1)} copy-done((bf16[256,16,128]{2,1,0:T(8,128)(2,1)S(1)}, bf16[256,16,128]{2,1,0:T(8,128)(2,1)}, u32[]{:S(2)}) %copy-start.2) | copy-done | bytes 1048600
  5.0 37.5 %shard_map.76 = (f32[4096,128]{1,0:T(8,128)S(1)}, f32[2,4,64,128]{3,2,1,0:T(8,128)S(1)}) custom-call(bf16[4096,128]{1,0:T(8,128)(2,1)S(1)} %bitcast.19, bf16[4096,128]{1,0:T(8,128)(2,1)S(1)} %bitcast.20, bf16[2,256,128]{2,1,0:T(8,128)(2,1)S(1)} %pad_maximum_fusion.kv_ref, s32[8]{0:T(128)S(1)} %select_reduce_fusion.wanted_ref, f32[4,8]{1,0:T(4,128)S(1)} %or_select_fusion.bias_ref), custom_call_target="tpu_custom_call" | custom-call | tf_op jit(solution)/shard_map/pallas_call | solution.py:251
  42.6 0.7 %copy.17 = f32[64,4,128]{2,1,0:T(4,128)} copy(f32[64,4,128]{2,0,1:T(8,128)S(1)} %get-tuple-element.18) | data formatting | bytes 262144
  43.3 0.7 %copy.16 = f32[64,4,128]{2,1,0:T(4,128)} copy(f32[64,4,128]{2,0,1:T(8,128)S(1)} %get-tuple-element.19) | data formatting | bytes 262144
  44.1 1.3 %copy.25 = f32[256,16,128]{2,1,0:T(8,128)} copy(f32[256,16,128]{2,1,0:T(8,128)S(1)} %bitcast.18) | data formatting | bytes 4194304
  (7 shorter events, 0.1 us)
Async XLA Ops:
  2.6 1.2 %copy-start.1 = (bf16[256,16,128]{2,1,0:T(8,128)(2,1)S(1)}, bf16[256,16,128]{2,1,0:T(8,128)(2,1)}, u32[]{:S(2)}) copy-start(bf16[256,16,128]{2,1,0:T(8,128)(2,1)} %param.5) | copy-start | bytes 3145732
  3.8 1.2 %copy-start.2 = (bf16[256,16,128]{2,1,0:T(8,128)(2,1)S(1)}, bf16[256,16,128]{2,1,0:T(8,128)(2,1)}, u32[]{:S(2)}) copy-start(bf16[256,16,128]{2,1,0:T(8,128)(2,1)} %param.8) | copy-start | bytes 3145732
  (1 other events, 0.0 us)

commit v2 on v1

--- a/solution.py
+++ b/solution.py
@@ -20,21 +20,24 @@
 
 def kernel(
     shards, peers, heads_dev, chunk,
-    q_hbm, go_hbm, kv_ref, wanted_ref, bias_ref,
+    q_hbm, go_hbm, kv_ref, wanted_ref, owner_ref, hit_ref, sel_ref,
     dq_hbm, out_ref,
-    q_buf, go_buf, dq_buf, slots, key_t, bias_buf, acc, own,
+    q_buf, go_buf, dq_buf, slots, key_mask, exp_buf, gp_buf, ds_buf,
+    top_buf, sum_buf, dot_buf, fac_buf, mean_buf, own,
     ask_out, ask_in, kv_out, ret_out, ret_in, hx_out, hx_in,
     load_sem, dq_sem, ask_ssem, ask_rsem, kv_ssem, kv_rsem,
     ret_ssem, ret_rsem, hx_ssem, hx_rsem,
 ):
     me = lax.axis_index("seq")
     mh = lax.axis_index("head")
-    width = q_hbm.shape[1]
+    width = q_hbm.shape[2]
     factor = width ** (-0.5)
+    scale = factor * math.log2(math.e)
     blocks = kv_ref.shape[1] // BLK
-    rows_b = q_buf.shape[0] // blocks
+    rows_b = q_buf.shape[1]
     part = kv_ref.shape[1] // peers
     run_total = HPG // heads_dev
+    cuts = rows_b // chunk
 
     def at_block(i):
         return pl.ds(pl.multiple_of(i * BLK, BLK), BLK)
@@ -86,9 +89,15 @@
     def _(i):
         ask_out[i] = jnp.full((8, 128), wanted_ref[i], jnp.int32)
 
-        @pl.when(i > me)
-        def _():
-            slots[:, at_block(i)] = jnp.zeros((2, BLK, width), BF16)
+        @pl.when(i >= me)
+        def _():
+            ds_buf[at_block(i)] = jnp.zeros((BLK, rows_b), BF16)
+            for b in range(blocks):
+                key_mask[b, at_block(i)] = jnp.zeros((BLK, width), BF16)
+
+    top_buf[...] = jnp.zeros(top_buf.shape, F32)
+    sum_buf[...] = jnp.zeros(sum_buf.shape, F32)
+    dot_buf[...] = jnp.zeros(dot_buf.shape, F32)
 
     pl.semaphore_wait(barrier, shards + peers - 2)
 
@@ -98,7 +107,45 @@
         def _():
             ask_copy(i, i, me).start()
 
-    acc[...] = jnp.zeros(acc.shape, F32)
+    def first_half(pair, block, keys, vals, causal):
+        for c in range(cuts):
+            lanes = slice(c * chunk, (c + 1) * chunk)
+            rows = slice(c * chunk, (c + 1) * chunk)
+            s = lax.dot_general(keys, q_buf[block, rows], NT, preferred_element_type=F32) * scale
+            if causal:
+                key_row = lax.broadcasted_iota(jnp.int32, (BLK, chunk), 0)
+                lane = lax.broadcasted_iota(jnp.int32, (BLK, chunk), 1)
+                s = jnp.where(key_row * heads_dev <= lane + c * chunk, s, NEG)
+            gp = lax.dot_general(vals, go_buf[block, rows], NT, preferred_element_type=F32)
+            top = jnp.max(s, axis=0, keepdims=True)
+            e = jnp.exp2(s - top)
+            exp_buf[pair, :, lanes] = e
+            gp_buf[pair, :, lanes] = gp
+            at = pl.ds(pair, 1)
+            top_buf[at, lanes] = top
+            sum_buf[at, lanes] = jnp.sum(e, axis=0, keepdims=True)
+            dot_buf[at, lanes] = jnp.sum(e * gp, axis=0, keepdims=True)
+
+    def second_half(pair, block, ds_at):
+        grad_key = jnp.zeros((BLK, width), F32)
+        grad_value = jnp.zeros((BLK, width), F32)
+        for c in range(cuts):
+            lanes = slice(c * chunk, (c + 1) * chunk)
+            rows = slice(c * chunk, (c + 1) * chunk)
+            at = pl.ds(pair, 1)
+            a = exp_buf[pair, :, lanes] * fac_buf[at, lanes]
+            ds = (a * (gp_buf[pair, :, lanes] - mean_buf[at, lanes])).astype(BF16)
+            ds_buf[ds_at, lanes] = ds
+            grad_value += jnp.dot(a.astype(BF16), go_buf[block, rows], preferred_element_type=F32)
+            grad_key += jnp.dot(ds, q_buf[block, rows], preferred_element_type=F32)
+        return grad_key * factor, grad_value
+
+    def own_first(b):
+        first_half(shards + b, b, kv_ref[0, at_block(b)], kv_ref[1, at_block(b)], True)
+
+    load_q.wait()
+    load_go.wait()
+    own_first(0)
 
     @pl.loop(0, shards)
     def _(i):
@@ -113,61 +160,65 @@
             kv_out[i] = total.astype(BF16)
             kv_copy(i, i, me).start()
 
-    load_q.wait()
-    load_go.wait()
+    @pl.loop(1, blocks)
+    def _(b):
+        own_first(b)
 
     @pl.loop(0, shards)
     def _(i):
         @pl.when(i < me)
         def _():
             kv_copy(i, i, i).wait_recv()
-
-    scale = factor * math.log2(math.e)
+            keys = slots[0, at_block(i)]
+            for b in range(blocks):
+                key_mask[b, at_block(i)] = (keys.astype(F32) * hit_ref[b, i]).astype(BF16)
+            first_half(i, owner_ref[i], keys, slots[1, at_block(i)], False)
+
+    fac = jnp.zeros((shards, rows_b), F32)
+    mean = jnp.zeros((shards, rows_b), F32)
+    for b in range(blocks):
+        at = slice(shards + b, shards + b + 1)
+        sel = sel_ref[b]
+        far = top_buf[0:shards] + sel
+        near = top_buf[at]
+        top = jnp.maximum(jnp.max(far, axis=0, keepdims=True), near)
+        far = jnp.exp2(far - top)
+        near = jnp.exp2(near - top)
+        inverse = 1.0 / (
+            jnp.sum(far * sum_buf[0:shards], axis=0, keepdims=True) + near * sum_buf[at]
+        )
+        row_dot = inverse * (
+            jnp.sum(far * dot_buf[0:shards], axis=0, keepdims=True) + near * dot_buf[at]
+        )
+        fac = fac + far * inverse
+        mean = mean + jnp.where(sel == 0.0, 1.0, 0.0) * row_dot
+        fac_buf[at] = near * inverse
+        mean_buf[at] = row_dot
+    fac_buf[0:shards] = fac
+    mean_buf[0:shards] = mean
+
+    @pl.loop(0, shards)
+    def _(i):
+        @pl.when(i < me)
+        def _():
+            grad_key, grad_value = second_half(i, owner_ref[i], at_block(i))
+            ret_out[i, 0] = grad_key.astype(BF16)
+            ret_out[i, 1] = grad_value.astype(BF16)
+            ret_copy(i, i, me).start()
 
     @pl.loop(0, blocks)
     def _(b):
-        slots[:, at_block(me)] = kv_ref[:, at_block(b)]
-        acc[:, at_block(me)] = jnp.zeros((2, BLK, width), F32)
-
-        @pl.loop(0, shards)
-        def _(i):
-            bias_buf[at_block(i)] = jnp.full((BLK, chunk), bias_ref[b, i], F32)
-
-        key_t[...] = slots[0].T
-
-        @pl.loop(0, rows_b // chunk)
-        def _(c):
-            rows = pl.ds(pl.multiple_of(b * rows_b + c * chunk, chunk), chunk)
-            key_row = lax.broadcasted_iota(jnp.int32, (BLK, chunk), 0)
-            lane = lax.broadcasted_iota(jnp.int32, (BLK, chunk), 1)
-            bias_buf[at_block(me)] = jnp.where(key_row * heads_dev <= lane + c * chunk, 0.0, NEG)
-            qc = q_buf[rows]
-            gc = go_buf[rows]
-            s = lax.dot_general(slots[0], qc, NT, preferred_element_type=F32)
-            s = s * scale + bias_buf[...]
-            p = jnp.exp2(s - jnp.max(s, axis=0, keepdims=True))
-            inverse = 1.0 / jnp.sum(p, axis=0, keepdims=True)
-            a = p * inverse
-            gp = lax.dot_general(slots[1], gc, NT, preferred_element_type=F32)
-            row_dot = jnp.sum(a * gp, axis=0, keepdims=True)
-            ds = (a * (gp - row_dot)).astype(BF16)
-            acc[1] += jnp.dot(a.astype(BF16), gc, preferred_element_type=F32)
-            acc[0] += jnp.dot(ds, qc, preferred_element_type=F32)
-            dq_t = jnp.dot(key_t[...], ds, preferred_element_type=F32)
-            dq_buf[rows] = (dq_t * factor).T
-
-        own[0, at_block(b)] = acc[0, at_block(me)] * factor
-        own[1, at_block(b)] = acc[1, at_block(me)]
-        rows = pl.ds(pl.multiple_of(b * rows_b, rows_b), rows_b)
-        pltpu.make_async_copy(dq_buf.at[rows], dq_hbm.at[rows], dq_sem.at[b]).start()
-
-    @pl.loop(0, shards)
-    def _(i):
-        @pl.when(i < me)
-        def _():
-            ret_out[i, 0] = (acc[0, at_block(i)] * factor).astype(BF16)
-            ret_out[i, 1] = acc[1, at_block(i)].astype(BF16)
-            ret_copy(i, i, me).start()
+        grad_key, grad_value = second_half(shards + b, b, at_block(shards + b))
+        own[0, at_block(b)] = grad_key
+        own[1, at_block(b)] = grad_value
+        far_t = key_mask[b].T
+        near_t = kv_ref[0, at_block(b)].T
+        for c in range(cuts):
+            lanes = slice(c * chunk, (c + 1) * chunk)
+            dq_t = jnp.dot(far_t, ds_buf[0 : shards * BLK, lanes], preferred_element_type=F32)
+            dq_t += jnp.dot(near_t, ds_buf[at_block(shards + b), lanes], preferred_element_type=F32)
+            dq_buf[b, lanes] = (dq_t * factor).T
+        pltpu.make_async_copy(dq_buf.at[b], dq_hbm.at[b], dq_sem.at[b]).start()
 
     @pl.loop(0, shards)
     def _(i):
@@ -220,8 +271,7 @@
 
     @pl.loop(0, blocks)
     def _(b):
-        rows = pl.ds(pl.multiple_of(b * rows_b, rows_b), rows_b)
-        pltpu.make_async_copy(dq_buf.at[rows], dq_hbm.at[rows], dq_sem.at[b]).wait()
+        pltpu.make_async_copy(dq_buf.at[b], dq_hbm.at[b], dq_sem.at[b]).wait()
 
 
 def on_device(queries, key_states, values, grad_out, picked_blocks):
@@ -229,7 +279,6 @@
     blocks = tokens_dev // BLK
     shards = lax.axis_size("seq")
     peers = lax.axis_size("head")
-    me = lax.axis_index("seq")
     group_id = lax.axis_index("head") // (HPG // heads_dev)
     kv = jnp.stack([
         lax.dynamic_index_in_dim(key_states, group_id, 1, keepdims=False),
@@ -239,11 +288,14 @@
     shard_ids = jnp.arange(shards, dtype=jnp.int32)
     match = (picks >= 0)[:, :, None] & ((picks // blocks)[:, :, None] == shard_ids)
     wanted = jnp.max(jnp.where(match, (picks % blocks)[:, :, None], -1), axis=(0, 1))
-    bias = jnp.where(jnp.any(match, axis=1) | (shard_ids == me), 0.0, NEG).astype(F32)
-    rows = tokens_dev * heads_dev
-    chunk = min(256, rows // blocks)
+    hit = jnp.any(match, axis=1)
+    block_ids = jnp.arange(blocks, dtype=jnp.int32)[:, None]
+    owner = jnp.max(jnp.where(hit, block_ids, 0), axis=0)
+    sel = jnp.where(hit, 0.0, NEG).astype(F32)[:, :, None]
+    rows_b = tokens_dev * heads_dev // blocks
+    chunk = min(512, rows_b)
     part = tokens_dev // peers
-    keys = shards * BLK
+    pairs = shards + blocks
     dma = pltpu.SemaphoreType.DMA
     any_spec = pl.BlockSpec(memory_space=pl.ANY)
     vmem = pl.BlockSpec(memory_space=pltpu.VMEM)
@@ -251,19 +303,25 @@
     dq, out = pl.pallas_call(
         functools.partial(kernel, shards, peers, heads_dev, chunk),
         out_shape=(
-            jax.ShapeDtypeStruct((rows, width), F32),
+            jax.ShapeDtypeStruct((blocks, rows_b, width), F32),
             jax.ShapeDtypeStruct((2, G, part, width), F32),
         ),
-        in_specs=[any_spec, any_spec, vmem, smem, smem],
+        in_specs=[any_spec, any_spec, vmem, smem, smem, smem, vmem],
         out_specs=(any_spec, vmem),
         scratch_shapes=[
-            pltpu.VMEM((rows, width), BF16),
-            pltpu.VMEM((rows, width), BF16),
-            pltpu.VMEM((rows, width), F32),
-            pltpu.VMEM((2, keys, width), BF16),
-            pltpu.VMEM((width, keys), BF16),
-            pltpu.VMEM((keys, chunk), F32),
-            pltpu.VMEM((2, keys, width), F32),
+            pltpu.VMEM((blocks, rows_b, width), BF16),
+            pltpu.VMEM((blocks, rows_b, width), BF16),
+            pltpu.VMEM((blocks, rows_b, width), F32),
+            pltpu.VMEM((2, shards * BLK, width), BF16),
+            pltpu.VMEM((blocks, shards * BLK, width), BF16),
+            pltpu.VMEM((pairs, BLK, rows_b), F32),
+            pltpu.VMEM((pairs, BLK, rows_b), F32),
+            pltpu.VMEM((pairs * BLK, rows_b), BF16),
+            pltpu.VMEM((pairs, rows_b), F32),
+            pltpu.VMEM((pairs, rows_b), F32),
+            pltpu.VMEM((pairs, rows_b), F32),
+            pltpu.VMEM((pairs, rows_b), F32),
+            pltpu.VMEM((pairs, rows_b), F32),
             pltpu.VMEM((2, tokens_dev, width), F32),
             pltpu.VMEM((shards, 8, 128), jnp.int32),
             pltpu.VMEM((shards, 8, 128), jnp.int32),
@@ -277,9 +335,12 @@
             dma((shards,)), dma((shards,)), dma((peers,)), dma((peers,)),
         ],
         compiler_params=pltpu.CompilerParams(
-            collective_id=0, has_side_effects=True, vmem_limit_bytes=48 * 1024 * 1024
+            collective_id=0, has_side_effects=True, vmem_limit_bytes=62 * 1024 * 1024
         ),
-    )(queries.reshape(rows, width), grad_out.reshape(rows, width), kv, wanted, bias)
+    )(
+        queries.reshape(blocks, rows_b, width), grad_out.reshape(blocks, rows_b, width), kv,
+        wanted, owner, hit.astype(F32), sel,
+    )
     return (
         dq.reshape(tokens_dev, heads_dev, width),
         out[0].transpose(1, 0, 2),

time: 45.6 us -> 37.8 us (0.83)
  Pallas kernels: 37.5 us -> 26.6 us
  other arithmetic: 0.53 us -> 2.81 us
  local copies, waits for them, and re-layouts: 6.62 us -> 7.56 us
    pallas_call x1, Pallas kernels: 37.5 us -> 26.6 us  [on_device(): pl.pallas_call(functools.partial(kernel, shards, peers, heads_dev, chunk)...]
    transpose x1, local copies, waits for them, and re-layouts: 0.02 us -> 0.99 us  [on_device(): out[1].transpose(1, 0, 2)]
    unnamed x11 -> x7, local copies, waits for them, and re-layouts: 5.28 us -> 4.56 us
    select_n x0 -> x1, local copies, waits for them, and re-layouts: none -> 0.7 us  [on_device(): sel = jnp.where(hit, 0.0, NEG).astype(F32)[:, :, None]]
    another operation x1, other arithmetic: 0.02 us -> 0.67 us  [on_device(): jnp.stack([lax.dynamic_index_in_dim(key_states, group_id, 1, keepdims=Fal...]
    convert_element_type x0 -> x1, other arithmetic: none -> 0.58 us  [on_device(): hit.astype(F32)]
    reduce_max x0 -> x1, other arithmetic: none -> 0.55 us  [on_device(): owner = jnp.max(jnp.where(hit, block_ids, 0), axis=0)]
    reduce_max x1, other arithmetic: 0.13 us -> 0.63 us  [on_device(): jnp.max(jnp.where(match, (picks % blocks)[:, :, None], -1), axis=(0, 1))]
where the time goes in v2:
time: 37.8 us; the launch traced here: 37.6 us
  Pallas kernels  26.6 us (70%)
  local copies, waits for them, and re-layouts  7.56 us (20%)
  other arithmetic  2.81 us (7%)
  between operations  0.69 us (2%)
    pallas_call x1, Pallas kernels, on_device(): pl.pallas_call(functools.partial(kernel, shards, peers, heads_dev, chunk)...  26.6 us
    unnamed x7, local copies, waits for them, and re-layouts  4.56 us
    dynamic_slice x1, local copies, waits for them, and re-layouts, on_device(): lax.dynamic_index_in_dim(values, group_id, 1, keepdims=False)  1.3 us
    transpose x1, local copies, waits for them, and re-layouts, on_device(): out[1].transpose(1, 0, 2)  0.99 us

profile of v2, /device:TPU:0, one launch (start us, length us, event | category | flops | bytes accessed | tf_op | source)
XLA Modules:
  0.0 37.6 jit_solution(9815266889768456568)
XLA Ops:
  0.6 0.0 copy-start
  0.6 0.0 copy-done
  0.7 0.1 slice_compare_fusion.1
  0.8 0.1 add_select_fusion.1
  0.8 0.1 add_select_fusion
  0.9 0.6 %select_reduce_fusion.wanted_ref = s32[8]{0:T(128)} fusion(s32[4,15]{1,0:T(4,128)S(1)} %add_select_fusion, s32[4,15]{1,0:T(4,128)S(1)} %get-tuple-element.16, pred[4,15]{1,0:T(4,128)(4,1)S(1)} %slice_compare_fusion.1), kind=kLoop, calls=%fused_computation.5 | loop fusion | flops 1912 | bytes 572 | tf_op jit(solution)/shard_map/reduce_max | solution.py:290
  1.5 0.1 fusion.1
  1.7 0.6 %select_reduce_fusion.1.owner_ref = s32[8]{0:T(128)} fusion(pred[4,8]{1,0:T(4,128)(4,1)S(1)} %fusion.1), kind=kLoop, calls=%fused_computation.15 | loop fusion | flops 56 | bytes 64 | tf_op jit(solution)/shard_map/reduce_max | solution.py:293
  2.2 0.6 %convert_element_type.3.hit_ref = f32[4,8]{1,0:T(4,128)} convert(pred[4,8]{1,0:T(4,128)(4,1)S(1)} %fusion.1) | non-fusion elementwise | flops 32 | bytes 160 | tf_op jit(solution)/shard_map/convert_element_type | solution.py:342
  2.8 0.7 %copy.18.sel_ref = f32[4,8,1]{2,1,0:T(8,128)} copy(f32[4,8,1]{1,0,2:T(4,128)S(1)} %select_bitcast_fusion) | data formatting | bytes 256 | tf_op jit(solution)/shard_map/jit(_where)/select_n | solution.py:294
  3.5 1.3 %constant_dynamic-slice_fusion.1 = (bf16[256,1,128]{2,1,0:T(2,128)(2,1)S(1)}, bf16[256,1,128]{2,1,0:T(2,128)(2,1)S(1)}) fusion(bf16[256,4,128]{2,1,0:T(4,128)(2,1)} %param.7, s32[]{:T(128)S(6)} %select_n.43, bf16[256,4,128]{2,1,0:T(4,128)(2,1)} %param.6), kind=kLoop, calls=%fused_computation.22 | loop fusion | bytes 262148 | tf_op jit(solution)/shard_map/jit(dynamic_index_in_dim)/dynamic_slice | solution.py:285
  4.9 0.7 %pad_maximum_fusion.kv_ref = bf16[2,256,128]{2,1,0:T(8,128)(2,1)} fusion(bf16[1,256,128]{2,1,0:T(8,128)(2,1)S(1)} %bitcast.23, bf16[1,256,128]{2,1,0:T(8,128)(2,1)S(1)} %bitcast.24), kind=kLoop, calls=%fused_computation | loop fusion | flops 65536 | bytes 262144 | tf_op jit(solution)/shard_map/stack | solution.py:283
  5.5 26.6 %shard_map.76 = (f32[4,1024,128]{2,1,0:T(8,128)}, f32[2,4,64,128]{3,2,1,0:T(8,128)}) custom-call(bf16[4,1024,128]{2,1,0:T(8,128)(2,1)} %bitcast.21, bf16[4,1024,128]{2,1,0:T(8,128)(2,1)} %bitcast.22, bf16[2,256,128]{2,1,0:T(8,128)(2,1)} %pad_maximum_fusion.kv_ref, s32[8]{0:T(128)} %select_reduce_fusion.wanted_ref, s32[8]{0:T(128)} %select_reduce_fusion.1.owner_ref, ...), custom_call_target="tpu_custom_call" | custom-call | tf_op jit(solution)/shard_map/pallas_call | solution.py:303
  32.1 1.0 %slice_bitcast_fusion = (f32[64,4,128]{2,0,1:T(8,128)S(1)}, f32[64,4,128]{2,0,1:T(8,128)S(1)}) fusion(f32[2,4,64,128]{3,2,1,0:T(8,128)} %get-tuple-element.6), kind=kLoop, calls=%fused_computation.1 | loop fusion | bytes 524288 | tf_op jit(solution)/shard_map/transpose | solution.py:347
  33.1 0.7 %copy.20 = f32[64,4,128]{2,1,0:T(4,128)} copy(f32[64,4,128]{2,0,1:T(8,128)S(1)} %get-tuple-element.18) | data formatting | bytes 262144
  33.8 0.7 %copy.19 = f32[64,4,128]{2,1,0:T(4,128)} copy(f32[64,4,128]{2,0,1:T(8,128)S(1)} %get-tuple-element.19) | data formatting | bytes 262144
  34.6 3.0 %copy.28 = f32[256,16,128]{2,1,0:T(8,128)} copy(f32[256,16,128]{2,1,0:T(8,128)} %bitcast.20) | data formatting | bytes 4194304
  (4 shorter events, 0.0 us)
Async XLA Ops:
  (1 other events, 0.0 us)

commit v3 on v2

--- a/solution.py
+++ b/solution.py
@@ -12,6 +12,7 @@
 HPG = 16
 BLK = 64
 NEG = -1e30
+FAR_UNROLL = 8
 MESH = pl.DeviceIdType.MESH
 F32 = jnp.float32
 BF16 = jnp.bfloat16
@@ -21,11 +22,11 @@
 def kernel(
     shards, peers, heads_dev, chunk,
     q_hbm, go_hbm, kv_ref, wanted_ref, owner_ref, hit_ref, sel_ref,
-    dq_hbm, out_ref,
-    q_buf, go_buf, dq_buf, slots, key_mask, exp_buf, gp_buf, ds_buf,
+    dq_ref, out_ref,
+    q_buf, go_buf, slots, key_mask, exp_buf, gp_buf, ds_buf,
     top_buf, sum_buf, dot_buf, fac_buf, mean_buf, own,
     ask_out, ask_in, kv_out, ret_out, ret_in, hx_out, hx_in,
-    load_sem, dq_sem, ask_ssem, ask_rsem, kv_ssem, kv_rsem,
+    load_sem, ask_ssem, ask_rsem, kv_ssem, kv_rsem,
     ret_ssem, ret_rsem, hx_ssem, hx_rsem,
 ):
     me = lax.axis_index("seq")
@@ -91,13 +92,7 @@
 
         @pl.when(i >= me)
         def _():
-            ds_buf[at_block(i)] = jnp.zeros((BLK, rows_b), BF16)
-            for b in range(blocks):
-                key_mask[b, at_block(i)] = jnp.zeros((BLK, width), BF16)
-
-    top_buf[...] = jnp.zeros(top_buf.shape, F32)
-    sum_buf[...] = jnp.zeros(sum_buf.shape, F32)
-    dot_buf[...] = jnp.zeros(dot_buf.shape, F32)
+            slots[:, at_block(i)] = jnp.zeros((2, BLK, width), BF16)
 
     pl.semaphore_wait(barrier, shards + peers - 2)
 
@@ -160,8 +155,7 @@
             kv_out[i] = total.astype(BF16)
             kv_copy(i, i, me).start()
 
-    @pl.loop(1, blocks)
-    def _(b):
+    for b in range(1, blocks):
         own_first(b)
 
     @pl.loop(0, shards)
@@ -169,10 +163,29 @@
         @pl.when(i < me)
         def _():
             kv_copy(i, i, i).wait_recv()
-            keys = slots[0, at_block(i)]
-            for b in range(blocks):
-                key_mask[b, at_block(i)] = (keys.astype(F32) * hit_ref[b, i]).astype(BF16)
-            first_half(i, owner_ref[i], keys, slots[1, at_block(i)], False)
+
+    def each_far(body):
+        if shards - 1 <= FAR_UNROLL:
+            for i in range(shards - 1):
+                body(i)
+        else:
+            pl.loop(0, shards - 1)(body)
+
+    def far_first(i):
+        keys = slots[0, at_block(i)]
+        for b in range(blocks):
+            key_mask[b, at_block(i)] = (keys.astype(F32) * hit_ref[b, i]).astype(BF16)
+        first_half(i, owner_ref[i], keys, slots[1, at_block(i)], False)
+
+    each_far(far_first)
+
+    last = shards - 1
+    top_buf[last : last + 1] = jnp.zeros((1, rows_b), F32)
+    sum_buf[last : last + 1] = jnp.zeros((1, rows_b), F32)
+    dot_buf[last : last + 1] = jnp.zeros((1, rows_b), F32)
+    ds_buf[at_block(last)] = jnp.zeros((BLK, rows_b), BF16)
+    for b in range(blocks):
+        key_mask[b, at_block(last)] = jnp.zeros((BLK, width), BF16)
 
     fac = jnp.zeros((shards, rows_b), F32)
     mean = jnp.zeros((shards, rows_b), F32)
@@ -197,17 +210,20 @@
     fac_buf[0:shards] = fac
     mean_buf[0:shards] = mean
 
+    def far_second(i):
+        grad_key, grad_value = second_half(i, owner_ref[i], at_block(i))
+        ret_out[i, 0] = grad_key.astype(BF16)
+        ret_out[i, 1] = grad_value.astype(BF16)
+
+    each_far(far_second)
+
     @pl.loop(0, shards)
     def _(i):
         @pl.when(i < me)
         def _():
-            grad_key, grad_value = second_half(i, owner_ref[i], at_block(i))
-            ret_out[i, 0] = grad_key.astype(BF16)
-            ret_out[i, 1] = grad_value.astype(BF16)
             ret_copy(i, i, me).start()
 
-    @pl.loop(0, blocks)
-    def _(b):
+    for b in range(blocks):
         grad_key, grad_value = second_half(shards + b, b, at_block(shards + b))
         own[0, at_block(b)] = grad_key
         own[1, at_block(b)] = grad_value
@@ -217,8 +233,7 @@
             lanes = slice(c * chunk, (c + 1) * chunk)
             dq_t = jnp.dot(far_t, ds_buf[0 : shards * BLK, lanes], preferred_element_type=F32)
             dq_t += jnp.dot(near_t, ds_buf[at_block(shards + b), lanes], preferred_element_type=F32)
-            dq_buf[b, lanes] = (dq_t * factor).T
-        pltpu.make_async_copy(dq_buf.at[b], dq_hbm.at[b], dq_sem.at[b]).start()
+            dq_ref[b, lanes] = (dq_t * factor).T.astype(BF16)
 
     @pl.loop(0, shards)
     def _(i):
@@ -268,10 +283,6 @@
         @pl.when(i != mh)
         def _():
             hx_copy(i, i, mh).wait_send()
-
-    @pl.loop(0, blocks)
-    def _(b):
-        pltpu.make_async_copy(dq_buf.at[b], dq_hbm.at[b], dq_sem.at[b]).wait()
 
 
 def on_device(queries, key_states, values, grad_out, picked_blocks):
@@ -297,21 +308,20 @@
     part = tokens_dev // peers
     pairs = shards + blocks
     dma = pltpu.SemaphoreType.DMA
-    any_spec = pl.BlockSpec(memory_space=pl.ANY)
+    hbm = pl.BlockSpec(memory_space=pltpu.HBM)
     vmem = pl.BlockSpec(memory_space=pltpu.VMEM)
     smem = pl.BlockSpec(memory_space=pltpu.SMEM)
     dq, out = pl.pallas_call(
         functools.partial(kernel, shards, peers, heads_dev, chunk),
         out_shape=(
-            jax.ShapeDtypeStruct((blocks, rows_b, width), F32),
+            jax.ShapeDtypeStruct((blocks, rows_b, width), BF16),
             jax.ShapeDtypeStruct((2, G, part, width), F32),
         ),
-        in_specs=[any_spec, any_spec, vmem, smem, smem, smem, vmem],
-        out_specs=(any_spec, vmem),
+        in_specs=[hbm, hbm, vmem, smem, smem, smem, vmem],
+        out_specs=(vmem, vmem),
         scratch_shapes=[
             pltpu.VMEM((blocks, rows_b, width), BF16),
             pltpu.VMEM((blocks, rows_b, width), BF16),
-            pltpu.VMEM((blocks, rows_b, width), F32),
             pltpu.VMEM((2, shards * BLK, width), BF16),
             pltpu.VMEM((blocks, shards * BLK, width), BF16),
             pltpu.VMEM((pairs, BLK, rows_b), F32),
@@ -330,19 +340,19 @@
             pltpu.VMEM((shards, 2, BLK, width), BF16),
             pltpu.VMEM((peers, 2, part, width), BF16),
             pltpu.VMEM((peers, 2, part, width), BF16),
-            dma((2,)), dma((blocks,)),
+            dma((2,)),
             dma((shards,)), dma((shards,)), dma((shards,)), dma((shards,)),
             dma((shards,)), dma((shards,)), dma((peers,)), dma((peers,)),
         ],
         compiler_params=pltpu.CompilerParams(
-            collective_id=0, has_side_effects=True, vmem_limit_bytes=62 * 1024 * 1024
+            collective_id=0, has_side_effects=True, vmem_limit_bytes=52 * 1024 * 1024
         ),
     )(
         queries.reshape(blocks, rows_b, width), grad_out.reshape(blocks, rows_b, width), kv,
         wanted, owner, hit.astype(F32), sel,
     )
     return (
-        dq.reshape(tokens_dev, heads_dev, width),
+        dq.reshape(tokens_dev, heads_dev, width).astype(F32),
         out[0].transpose(1, 0, 2),
         out[1].transpose(1, 0, 2),
     )

time: 37.8 us -> 31.2 us (0.83)
  local copies, waits for them, and re-layouts: 7.56 us -> 2.95 us
  Pallas kernels: 26.6 us -> 25.4 us
  other arithmetic: 2.81 us -> 2.03 us
    unnamed x7 -> x6, local copies, waits for them, and re-layouts: 4.56 us -> 1.52 us
    convert_element_type x0 -> x1, other arithmetic: none -> 1.48 us  [on_device(): dq.reshape(tokens_dev, heads_dev, width).astype(F32)]
    pallas_call x1, Pallas kernels: 26.6 us -> 25.4 us  [on_device(): pl.pallas_call(functools.partial(kernel, shards, peers, heads_dev, chunk)...]
    transpose x1, local copies, waits for them, and re-layouts: 0.99 us -> 0.02 us  [on_device(): out[1].transpose(1, 0, 2)]
    another operation x1, other arithmetic: 0.67 us -> 0.02 us  [on_device(): jnp.stack([lax.dynamic_index_in_dim(key_states, group_id, 1, keepdims=Fal...]
    select_n x1, local copies, waits for them, and re-layouts: 0.7 us -> 0.1 us  [on_device(): sel = jnp.where(hit, 0.0, NEG).astype(F32)[:, :, None]]
    convert_element_type x1, other arithmetic: 0.58 us -> 0.01 us  [on_device(): hit.astype(F32)]
    reduce_max x1, other arithmetic: 0.55 us -> 0.02 us  [on_device(): owner = jnp.max(jnp.where(hit, block_ids, 0), axis=0)]
where the time goes in v3:
time: 31.2 us; the launch traced here: 31.1 us
  Pallas kernels  25.4 us (81%)
  local copies, waits for them, and re-layouts  2.95 us (9%)
  other arithmetic  2.03 us (7%)
  between operations  0.72 us (2%)
    pallas_call x1, Pallas kernels, on_device(): pl.pallas_call(functools.partial(kernel, shards, peers, heads_dev, chunk)...  25.4 us
    unnamed x6, local copies, waits for them, and re-layouts  1.52 us
    convert_element_type x1, other arithmetic, on_device(): dq.reshape(tokens_dev, heads_dev, width).astype(F32)  1.48 us
    dynamic_slice x1, local copies, waits for them, and re-layouts, on_device(): lax.dynamic_index_in_dim(values, group_id, 1, keepdims=False)  1.3 us

profile of v3, /device:TPU:0, one launch (start us, length us, event | category | flops | bytes accessed | tf_op | source)
XLA Modules:
  0.0 31.1 jit_solution(11584184993293179246)
XLA Ops:
  0.6 0.0 copy-start
  0.6 0.0 copy-done
  0.7 0.1 slice_compare_fusion.1
  0.8 0.1 add_select_fusion.1
  0.8 0.1 add_select_fusion
  0.9 0.1 select_reduce_fusion.wanted_ref
  1.0 0.1 fusion.1
  1.2 0.1 copy.18.sel_ref
  1.3 1.3 %constant_dynamic-slice_fusion.1 = (bf16[256,1,128]{2,1,0:T(2,128)(2,1)S(1)}, bf16[256,1,128]{2,1,0:T(2,128)(2,1)S(1)}) fusion(bf16[256,4,128]{2,1,0:T(4,128)(2,1)} %param.7, s32[]{:T(128)S(6)} %select_n.43, bf16[256,4,128]{2,1,0:T(4,128)(2,1)} %param.6), kind=kLoop, calls=%fused_computation.22 | loop fusion | bytes 262148 | tf_op jit(solution)/shard_map/jit(dynamic_index_in_dim)/dynamic_slice | solution.py:296
  2.7 25.4 %shard_map.76 = (bf16[4,1024,128]{2,1,0:T(8,128)(2,1)S(1)}, f32[2,4,64,128]{3,2,1,0:T(8,128)S(1)}) custom-call(bf16[4,1024,128]{2,1,0:T(8,128)(2,1)} %bitcast.22, bf16[4,1024,128]{2,1,0:T(8,128)(2,1)} %bitcast.23, bf16[2,256,128]{2,1,0:T(8,128)(2,1)S(1)} %pad_maximum_fusion.kv_ref, s32[8]{0:T(128)S(1)} %select_reduce_fusion.wanted_ref, ...), custom_call_target="tpu_custom_call" | custom-call | tf_op jit(solution)/shard_map/pallas_call | solution.py:314
  28.1 0.7 %copy.20 = f32[64,4,128]{2,1,0:T(4,128)} copy(f32[64,4,128]{2,0,1:T(8,128)S(1)} %get-tuple-element.18) | data formatting | bytes 262144
  28.9 0.7 %copy.19 = f32[64,4,128]{2,1,0:T(4,128)} copy(f32[64,4,128]{2,0,1:T(8,128)S(1)} %get-tuple-element.19) | data formatting | bytes 262144
  29.6 1.5 %convert.1 = f32[256,16,128]{2,1,0:T(8,128)} convert(bf16[256,16,128]{2,1,0:T(8,128)(2,1)S(1)} %bitcast.21) | non-fusion elementwise | flops 524288 | bytes 3145728 | tf_op jit(solution)/shard_map/convert_element_type | solution.py:355
  (8 shorter events, 0.1 us)
Async XLA Ops:
  (1 other events, 0.0 us)

commit v4 on v3

--- a/solution.py
+++ b/solution.py
@@ -215,13 +215,24 @@
         ret_out[i, 0] = grad_key.astype(BF16)
         ret_out[i, 1] = grad_value.astype(BF16)
 
-    each_far(far_second)
-
-    @pl.loop(0, shards)
-    def _(i):
+    def send_back(i):
         @pl.when(i < me)
         def _():
             ret_copy(i, i, me).start()
+
+    if shards - 1 <= FAR_UNROLL:
+        for start in range(0, shards - 1, 2):
+            group = range(start, min(start + 2, shards - 1))
+            for i in group:
+                far_second(i)
+            for i in group:
+                send_back(i)
+    else:
+
+        @pl.loop(0, shards - 1)
+        def _(i):
+            far_second(i)
+            send_back(i)
 
     for b in range(blocks):
         grad_key, grad_value = second_half(shards + b, b, at_block(shards + b))
@@ -265,7 +276,8 @@
         total = hx_in[g * run_total].astype(F32)
         for c in range(1, run_total):
             total = total + hx_in[g * run_total + c].astype(F32)
-        out_ref[:, g] = total
+        for t in range(2):
+            out_ref[t, :, g, :] = total[t]
 
     @pl.loop(0, shards)
     def _(i):
@@ -315,7 +327,7 @@
         functools.partial(kernel, shards, peers, heads_dev, chunk),
         out_shape=(
             jax.ShapeDtypeStruct((blocks, rows_b, width), BF16),
-            jax.ShapeDtypeStruct((2, G, part, width), F32),
+            jax.ShapeDtypeStruct((2, part, G, width), F32),
         ),
         in_specs=[hbm, hbm, vmem, smem, smem, smem, vmem],
         out_specs=(vmem, vmem),
@@ -353,8 +365,8 @@
     )
     return (
         dq.reshape(tokens_dev, heads_dev, width).astype(F32),
-        out[0].transpose(1, 0, 2),
-        out[1].transpose(1, 0, 2),
+        out[0],
+        out[1],
     )
 
 

time: 31.2 us -> 30.2 us (0.968)
  local copies, waits for them, and re-layouts: 2.95 us -> 2.16 us
    unnamed x6 -> x4, local copies, waits for them, and re-layouts: 1.52 us -> 0.03 us
    squeeze x0 -> x1, local copies, waits for them, and re-layouts: none -> 0.72 us  [on_device(): out[1]]
where the time goes in v4:
time: 30.2 us; the launch traced here: 30 us
  Pallas kernels  25.1 us (83%)
  local copies, waits for them, and re-layouts  2.16 us (7%)
  other arithmetic  2.03 us (7%)
  between operations  0.71 us (2%)
    pallas_call x1, Pallas kernels, on_device(): pl.pallas_call(functools.partial(kernel, shards, peers, heads_dev, chunk)...  25.1 us
    convert_element_type x1, other arithmetic, on_device(): dq.reshape(tokens_dev, heads_dev, width).astype(F32)  1.48 us
    dynamic_slice x1, local copies, waits for them, and re-layouts, on_device(): lax.dynamic_index_in_dim(values, group_id, 1, keepdims=False)  1.3 us
    squeeze x1, local copies, waits for them, and re-layouts, on_device(): out[1]  0.72 us

profile of v4, /device:TPU:0, one launch (start us, length us, event | category | flops | bytes accessed | tf_op | source)
XLA Modules:
  0.0 30.0 jit_solution(10261325989521018693)
XLA Ops:
  0.6 0.0 copy-start
  0.6 0.0 copy-done
  0.7 0.1 slice_compare_fusion.1
  0.8 0.1 add_select_fusion.1
  0.8 0.1 add_select_fusion
  0.9 0.1 select_reduce_fusion.wanted_ref
  1.0 0.1 fusion.1
  1.2 0.1 copy.14.sel_ref
  1.3 1.3 %constant_dynamic-slice_fusion.1 = (bf16[256,1,128]{2,1,0:T(2,128)(2,1)S(1)}, bf16[256,1,128]{2,1,0:T(2,128)(2,1)S(1)}) fusion(bf16[256,4,128]{2,1,0:T(4,128)(2,1)} %param.7, s32[]{:T(128)S(6)} %select_n.43, bf16[256,4,128]{2,1,0:T(4,128)(2,1)} %param.6), kind=kLoop, calls=%fused_computation.22 | loop fusion | bytes 262148 | tf_op jit(solution)/shard_map/jit(dynamic_index_in_dim)/dynamic_slice | solution.py:308
  2.7 25.1 %shard_map.76 = (bf16[4,1024,128]{2,1,0:T(8,128)(2,1)S(1)}, f32[2,64,4,128]{3,2,1,0:T(4,128)S(1)}) custom-call(bf16[4,1024,128]{2,1,0:T(8,128)(2,1)} %bitcast.18, bf16[4,1024,128]{2,1,0:T(8,128)(2,1)} %bitcast.19, bf16[2,256,128]{2,1,0:T(8,128)(2,1)S(1)} %pad_maximum_fusion.kv_ref, s32[8]{0:T(128)S(1)} %select_reduce_fusion.wanted_ref, ...), custom_call_target="tpu_custom_call" | custom-call | tf_op jit(solution)/shard_map/pallas_call | solution.py:326
  27.8 0.7 %slice_bitcast_fusion = (f32[64,4,128]{2,1,0:T(4,128)}, f32[64,4,128]{2,1,0:T(4,128)}) fusion(f32[2,64,4,128]{3,2,1,0:T(4,128)S(1)} %get-tuple-element.6), kind=kLoop, calls=%fused_computation.1 | loop fusion | bytes 524288 | tf_op jit(solution)/shard_map/squeeze | solution.py:369
  28.5 1.5 %convert.1 = f32[256,16,128]{2,1,0:T(8,128)} convert(bf16[256,16,128]{2,1,0:T(8,128)(2,1)S(1)} %bitcast.17) | non-fusion elementwise | flops 524288 | bytes 3145728 | tf_op jit(solution)/shard_map/convert_element_type | solution.py:367
  (7 shorter events, 0.1 us)
Async XLA Ops:
  (1 other events, 0.0 us)
